TPU v7x, 32 devices: a whole 2x2x4 slice. The times are simulated.
32 devices in a mesh: grp: 2 (over x), dom: 16 (over z, y, core).
Axes of the slice: x: 2, y: 2, z: 4, core: 2. Of those that a mesh axis runs over, the one named last changes fastest.
Arguments:
- features: bfloat16 [24576, 128], P(('grp', 'dom')), parts along dimension 0, may hold values from -6 to 6
- block_tiles: bfloat16 [192, 128, 44, 128], P(('grp', 'dom')), parts along dimension 0, may hold values from -0.078125 to 0.078125
- block_cols: int32 [192, 44], P(('grp', 'dom')), parts along dimension 0, may hold values from 0 to 21, as said below
- halo_request: int32 [32, 16], P(('grp', 'dom')), parts along dimension 0, may hold values from 0 to 5
- labels: int32 [24576], P(('grp', 'dom')), parts along dimension 0, may hold values from 0 to 171
- weight_one: bfloat16 [128, 256], replicated, may hold values from -0.5 to 0.5
- weight_two: bfloat16 [256, 172], replicated, may hold values from -0.375 to 0.375
Outputs:
- logits: float32 [24576, 172], P(('grp', 'dom')), parts along dimension 0
- grad_one: float32 [256, 256], P('grp'), parts along dimension 0
- grad_two: float32 [512, 172], P('grp'), parts along dimension 0
There are 2 independent parts, one for each index of `grp`. A program takes and returns all parts, laid end to end along the dimension named above; an argument that names none is the same for every part. Nothing has to cross between parts.
Inputs may be any that keep to these rules, and one draw needn't show every extreme that they name: `block_cols`: among the 264 entries of each partition's block rows, every table entry 0 to 21 appears.
All inputs are finite; a program needn't handle non-finite values.
Results may differ from a plain program's by a relative error of at most 0.0039.
The roundings to bfloat16 on the way count: a program that leaves them out, or rounds other values in their place, can miss the bound.
Values may be sent and summed in bfloat16 or wider, within the bound.
A program may use at most 128 MiB of HBM per device.

v0:
```python
import math

import jax
import jax.numpy as jnp
from jax import lax
from jax.sharding import PartitionSpec as P


def split_parts(value):
    high = lax.optimization_barrier(value.astype(jnp.bfloat16))
    low = (value - high.astype(jnp.float32)).astype(jnp.bfloat16)
    return (high, low)


def dot_right(left, value):
    high, low = split_parts(value)
    return jnp.dot(left, high, preferred_element_type=jnp.float32) + jnp.dot(
        left, low, preferred_element_type=jnp.float32
    )


def dot_left(value, right):
    high, low = split_parts(value)
    return jnp.dot(high, right, preferred_element_type=jnp.float32) + jnp.dot(
        low, right, preferred_element_type=jnp.float32
    )


def aggregate_rows(block_tiles, block_cols, table, exact):
    count = block_cols.shape[0]
    kr_count = block_cols.shape[1]
    block_size = block_tiles.shape[1]
    width = table.shape[2]

    def one_row(index):
        taken = table[block_cols[index]].reshape(kr_count * block_size, width)
        tile = block_tiles[index].reshape(block_size, kr_count * block_size)
        if exact:
            return dot_right(tile, taken)
        return jnp.dot(tile, taken, preferred_element_type=jnp.float32)

    rows = lax.map(one_row, jnp.arange(count, dtype=jnp.int32))
    return rows.reshape(count * block_size, width)


def local(features, block_tiles, block_cols, halo_request, labels, weight_one, weight_two):
    parts = lax.axis_size("dom")
    count = block_cols.shape[0]
    kr_count = block_cols.shape[1]
    block_size = block_tiles.shape[1]
    classes = weight_two.shape[1]
    table_size = count + parts
    nodes = parts * count * block_size
    wanted = lax.all_to_all(
        halo_request.reshape(parts, 1), "dom", split_axis=0, concat_axis=0, tiled=True
    ).reshape(parts)
    own_blocks = features.reshape(count, block_size, features.shape[1])
    received = lax.all_to_all(own_blocks[wanted], "dom", split_axis=0, concat_axis=0, tiled=True)
    table = jnp.concatenate([own_blocks, received], axis=0)
    aggregated = aggregate_rows(block_tiles, block_cols, table, False).astype(jnp.bfloat16)
    pre_one = jnp.dot(aggregated, weight_one, preferred_element_type=jnp.float32)
    hidden = jnp.maximum(pre_one, 0.0).astype(jnp.bfloat16)
    product = jnp.dot(hidden, weight_two, preferred_element_type=jnp.float32)
    product_blocks = product.reshape(count, block_size, classes)
    taken = lax.all_to_all(
        product_blocks[wanted].astype(jnp.bfloat16), "dom", split_axis=0, concat_axis=0, tiled=True
    ).astype(jnp.float32)
    second_table = jnp.concatenate([product_blocks, taken], axis=0)
    logits = aggregate_rows(block_tiles, block_cols, second_table, True)
    top = jnp.max(logits, axis=1, keepdims=True)
    expo = jnp.exp(logits - top)
    probs = expo / jnp.sum(expo, axis=1, keepdims=True)
    onehot = (labels[:, None] == jnp.arange(classes, dtype=jnp.int32)[None, :]).astype(jnp.float32)
    grad_logits = (probs - onehot) / math.sqrt(nodes)
    grad_blocks = grad_logits.reshape(count, block_size, classes)

    def back_row(carry, index):
        tile = block_tiles[index].reshape(block_size, kr_count * block_size)
        terms = dot_right(tile.T, grad_blocks[index]).reshape(kr_count, block_size, classes)
        return (carry.at[block_cols[index]].add(terms), None)

    start = jnp.zeros((table_size, block_size, classes), jnp.float32)
    table_grads, _ = lax.scan(back_row, start, jnp.arange(count, dtype=jnp.int32))
    returned = lax.all_to_all(
        table_grads[count:].astype(jnp.bfloat16), "dom", split_axis=0, concat_axis=0, tiled=True
    ).astype(jnp.float32)
    gathered_back = jax.ops.segment_sum(returned, wanted, num_segments=count)
    grad_product = (table_grads[:count] + gathered_back).reshape(count * block_size, classes)
    grad_two_local = dot_right(hidden.T, grad_product)
    grad_two = lax.psum(grad_two_local, "dom")
    grad_hidden = dot_left(grad_product, weight_two.T)
    grad_pre = jnp.where(pre_one > 0.0, grad_hidden, 0.0)
    grad_one_local = dot_right(aggregated.T, grad_pre)
    grad_one = lax.psum(grad_one_local, "dom")
    return (logits, grad_one, grad_two)


def solution(mesh):
    placed = (
        P(("grp", "dom"), None),
        P(("grp", "dom"), None, None, None),
        P(("grp", "dom"), None),
        P(("grp", "dom"), None),
        P(("grp", "dom")),
        P(),
        P(),
    )
    return jax.shard_map(
        local,
        mesh=mesh,
        in_specs=placed,
        out_specs=(P(("grp", "dom"), None), P("grp", None), P("grp", None)),
        check_vma=False,
    )
```

profile of v0, /device:TPU:0, one launch (start us, length us, event | category | flops | bytes accessed | tf_op | source)
XLA Modules:
  0.0 492.2 jit_solution(17865255058534984724)
XLA Ops:
  7.9 13.6 %all_to_all.27 = s32[16,1,1]{2,1,0:T(1,128)S(1)} all-to-all(s32[16,1,1]{2,1,0:T(1,128)S(1)} %copy.36), channel_id=1, replica_groups=mesh['grp'=2,'dom'=16] {'dom'}, dimensions={0} | all-to-all | bytes 128 | tf_op jit(solution)/shard_map/all_to_all | solution.py:54
  21.9 2.3 gather_fusion.2
  24.3 3.6 all-to-all-start.1
  27.9 12.4 %copy.40 = bf16[6,128,44,128]{1,3,2,0:T(8,128)(2,1)} copy(bf16[6,128,44,128]{3,1,2,0:T(8,128)(2,1)} %param.14) | data formatting | bytes 17301504 | tf_op jit(solution)/shard_map/while | solution.py:42
  40.3 2.0 all-to-all-done.1
  42.4 37.0 %while.30 = (s32[]{:T(128)}, bf16[6,128,128]{2,1,0:T(8,128)(2,1)S(1)}, s32[6]{0:T(128)S(1)}, bf16[6,128,44,128]{1,3,2,0:T(8,128)(2,1)}, s32[6,44]{1,0:T(8,128)},...) while((s32[]{:T(128)}, bf16[6,128,128]{2,1,0:T(8,128)(2,1)S(1)}, ...), condition=%wide.region_1.2_spmd, body=%wide.region_0.1_spmd.sunk | while | flops 184550528 | bytes 8721239 | solution.py:42
  46.4 1.5 constant_dynamic-slice_fusion.9
  65.0 1.5 constant_dynamic-slice_fusion.9
  71.1 1.5 constant_dynamic-slice_fusion.9
  77.3 1.5 constant_dynamic-slice_fusion.9
  81.1 1.6 gather_fusion.3
  82.6 4.0 all-to-all-start.2
  86.7 17.6 %all-to-all-done.2 = bf16[16,128,172]{1,2,0:T(8,128)(2,1)S(1)} async-done(((bf16[16,128,172]{1,2,0:T(8,128)(2,1)}), bf16[16,128,172]{1,2,0:T(8,128)(2,1)S(1)}, u32[]{:S(2)}, u32[]{:S(2)}) %all-to-all-start.2) | async-done | bytes 704544 | tf_op jit(solution)/shard_map/all_to_all | solution.py:65
  104.4 1.5 pad_maximum_fusion
  105.9 2.1 copy.41
  108.0 93.8 %while.31 = (s32[]{:T(128)}, f32[6,128,172]{1,2,0:T(8,128)S(1)}, s32[6]{0:T(128)S(1)}, bf16[6,128,44,128]{1,3,2,0:T(8,128)(2,1)}, s32[6,44]{1,0:T(8,128)}, /*ind...) while((s32[]{:T(128)}, f32[6,128,172]{1,2,0:T(8,128)S(1)}, s32[6]{0:T(128)S(1)}, ...), condition=%wide.region_3.4_spmd, body=%wide.region_2.3_spmd.sunk | while | flops 499874432 | bytes 47672180 | solution.py:42
  111.0 3.5 gather_fusion.1
  114.5 3.1 bitcast_convert_fusion.4
  120.2 1.5 constant_dynamic-slice_fusion.10
  126.7 3.5 gather_fusion.1
  130.1 3.1 bitcast_convert_fusion.4
  135.8 1.5 constant_dynamic-slice_fusion.10
  142.3 3.5 gather_fusion.1
  145.7 3.1 bitcast_convert_fusion.4
  157.9 3.5 gather_fusion.1
  161.4 3.1 bitcast_convert_fusion.4
  173.5 3.5 gather_fusion.1
  177.0 3.1 bitcast_convert_fusion.4
  182.7 1.5 constant_dynamic-slice_fusion.10
  189.2 3.5 gather_fusion.1
  192.6 3.1 bitcast_convert_fusion.4
  202.1 3.2 fusion.16
  205.5 155.4 %while.32 = (s32[]{:T(128)}, f32[22,128,172]{1,2,0:T(8,128)S(1)}, s32[6]{0:T(128)S(1)}, s32[6,44]{1,0:T(8,128)}, bf16[6,128,44,128]{1,3,2,0:T(8,128)(2,1)}, /*in...) while((s32[]{:T(128)}, f32[22,128,172]{1,2,0:T(8,128)S(1)}, s32[6]{0:T(128)S(1)}, ...), condition=%wide.region_8.9_spmd, body=%wide.region_6.8_spmd.sunk | while | flops 497980032 | bytes 44934824 | solution.py:83
  210.3 2.6 convolution_add_fusion.6
  212.8 4.9 %reshape.244 = f32[44,128,172]{1,0,2:T(8,128)} reshape(f32[5632,172]{0,1:T(8,128)} %convolution_add_fusion.6) | data formatting | bytes 7749632 | tf_op jit(solution)/shard_map/while/body/eval_jaxpr/reshape | solution.py:79
  217.8 5.3 %copy.53 = f32[44,128,172]{1,2,0:T(8,128)} copy(f32[44,128,172]{1,0,2:T(8,128)} %reshape.244) | data formatting | bytes 7749632 | tf_op jit(solution)/shard_map/while/body/eval_jaxpr/reshape | solution.py:79
  223.8 7.6 %scatter_fusion = f32[22,128,172]{1,2,0:T(8,128)S(1)} fusion(f32[22,128,172]{1,2,0:T(8,128)S(1)} %get-tuple-element.371, s32[44]{0:T(128)S(1)} %fusion.82, f32[44,128,172]{1,2,0:T(8,128)} %copy.53), kind=kCustom, calls=%fused_computation.4.clone.1 | custom fusion | flops 968704 | bytes 11624624 | tf_op jit(solution)/shard_map/while/body/eval_jaxpr/scatter-add | solution.py:80
  234.0 1.5 constant_dynamic-slice_fusion.11
  236.2 2.6 convolution_add_fusion.6
  238.7 4.9 %reshape.244 = f32[44,128,172]{1,0,2:T(8,128)} reshape(f32[5632,172]{0,1:T(8,128)} %convolution_add_fusion.6) | data formatting | bytes 7749632 | tf_op jit(solution)/shard_map/while/body/eval_jaxpr/reshape | solution.py:79
  243.7 5.3 %copy.53 = f32[44,128,172]{1,2,0:T(8,128)} copy(f32[44,128,172]{1,0,2:T(8,128)} %reshape.244) | data formatting | bytes 7749632 | tf_op jit(solution)/shard_map/while/body/eval_jaxpr/reshape | solution.py:79
  249.7 7.6 %scatter_fusion = f32[22,128,172]{1,2,0:T(8,128)S(1)} fusion(f32[22,128,172]{1,2,0:T(8,128)S(1)} %get-tuple-element.371, s32[44]{0:T(128)S(1)} %fusion.82, f32[44,128,172]{1,2,0:T(8,128)} %copy.53), kind=kCustom, calls=%fused_computation.4.clone.1 | custom fusion | flops 968704 | bytes 11624624 | tf_op jit(solution)/shard_map/while/body/eval_jaxpr/scatter-add | solution.py:80
  262.1 2.6 convolution_add_fusion.6
  264.6 4.9 %reshape.244 = f32[44,128,172]{1,0,2:T(8,128)} reshape(f32[5632,172]{0,1:T(8,128)} %convolution_add_fusion.6) | data formatting | bytes 7749632 | tf_op jit(solution)/shard_map/while/body/eval_jaxpr/reshape | solution.py:79
  269.6 5.3 %copy.53 = f32[44,128,172]{1,2,0:T(8,128)} copy(f32[44,128,172]{1,0,2:T(8,128)} %reshape.244) | data formatting | bytes 7749632 | tf_op jit(solution)/shard_map/while/body/eval_jaxpr/reshape | solution.py:79
  275.6 7.6 %scatter_fusion = f32[22,128,172]{1,2,0:T(8,128)S(1)} fusion(f32[22,128,172]{1,2,0:T(8,128)S(1)} %get-tuple-element.371, s32[44]{0:T(128)S(1)} %fusion.82, f32[44,128,172]{1,2,0:T(8,128)} %copy.53), kind=kCustom, calls=%fused_computation.4.clone.1 | custom fusion | flops 968704 | bytes 11624624 | tf_op jit(solution)/shard_map/while/body/eval_jaxpr/scatter-add | solution.py:80
  288.0 2.6 convolution_add_fusion.6
  290.5 4.9 %reshape.244 = f32[44,128,172]{1,0,2:T(8,128)} reshape(f32[5632,172]{0,1:T(8,128)} %convolution_add_fusion.6) | data formatting | bytes 7749632 | tf_op jit(solution)/shard_map/while/body/eval_jaxpr/reshape | solution.py:79
  295.5 5.3 %copy.53 = f32[44,128,172]{1,2,0:T(8,128)} copy(f32[44,128,172]{1,0,2:T(8,128)} %reshape.244) | data formatting | bytes 7749632 | tf_op jit(solution)/shard_map/while/body/eval_jaxpr/reshape | solution.py:79
  301.5 7.6 %scatter_fusion = f32[22,128,172]{1,2,0:T(8,128)S(1)} fusion(f32[22,128,172]{1,2,0:T(8,128)S(1)} %get-tuple-element.371, s32[44]{0:T(128)S(1)} %fusion.82, f32[44,128,172]{1,2,0:T(8,128)} %copy.53), kind=kCustom, calls=%fused_computation.4.clone.1 | custom fusion | flops 968704 | bytes 11624624 | tf_op jit(solution)/shard_map/while/body/eval_jaxpr/scatter-add | solution.py:80
  313.9 2.6 convolution_add_fusion.6
  316.4 4.9 %reshape.244 = f32[44,128,172]{1,0,2:T(8,128)} reshape(f32[5632,172]{0,1:T(8,128)} %convolution_add_fusion.6) | data formatting | bytes 7749632 | tf_op jit(solution)/shard_map/while/body/eval_jaxpr/reshape | solution.py:79
  321.4 5.3 %copy.53 = f32[44,128,172]{1,2,0:T(8,128)} copy(f32[44,128,172]{1,0,2:T(8,128)} %reshape.244) | data formatting | bytes 7749632 | tf_op jit(solution)/shard_map/while/body/eval_jaxpr/reshape | solution.py:79
  327.4 7.6 %scatter_fusion = f32[22,128,172]{1,2,0:T(8,128)S(1)} fusion(f32[22,128,172]{1,2,0:T(8,128)S(1)} %get-tuple-element.371, s32[44]{0:T(128)S(1)} %fusion.82, f32[44,128,172]{1,2,0:T(8,128)} %copy.53), kind=kCustom, calls=%fused_computation.4.clone.1 | custom fusion | flops 968704 | bytes 11624624 | tf_op jit(solution)/shard_map/while/body/eval_jaxpr/scatter-add | solution.py:80
  339.8 2.6 convolution_add_fusion.6
  342.3 4.9 %reshape.244 = f32[44,128,172]{1,0,2:T(8,128)} reshape(f32[5632,172]{0,1:T(8,128)} %convolution_add_fusion.6) | data formatting | bytes 7749632 | tf_op jit(solution)/shard_map/while/body/eval_jaxpr/reshape | solution.py:79
  347.3 5.3 %copy.53 = f32[44,128,172]{1,2,0:T(8,128)} copy(f32[44,128,172]{1,0,2:T(8,128)} %reshape.244) | data formatting | bytes 7749632 | tf_op jit(solution)/shard_map/while/body/eval_jaxpr/reshape | solution.py:79
  353.3 7.6 %scatter_fusion = f32[22,128,172]{1,2,0:T(8,128)S(1)} fusion(f32[22,128,172]{1,2,0:T(8,128)S(1)} %get-tuple-element.371, s32[44]{0:T(128)S(1)} %fusion.82, f32[44,128,172]{1,2,0:T(8,128)} %copy.53), kind=kCustom, calls=%fused_computation.4.clone.1 | custom fusion | flops 968704 | bytes 11624624 | tf_op jit(solution)/shard_map/while/body/eval_jaxpr/scatter-add | solution.py:80
  361.9 5.2 %all-to-all-start.3 = ((bf16[16,128,172]{1,2,0:T(8,128)(2,1)}), bf16[16,128,172]{1,2,0:T(8,128)(2,1)}, u32[]{:S(2)}, u32[]{:S(2)}) async-start(bf16[16,128,172]{1,2,0:T(8,128)(2,1)} %slice.19), calls=%async_computation.3 | async-start | bytes 1441792 | tf_op jit(solution)/shard_map/all_to_all | solution.py:84
  367.4 17.4 %all-to-all-done.3 = bf16[16,128,172]{1,2,0:T(8,128)(2,1)} async-done(((bf16[16,128,172]{1,2,0:T(8,128)(2,1)}), bf16[16,128,172]{1,2,0:T(8,128)(2,1)}, u32[]{:S(2)}, u32[]{:S(2)}) %all-to-all-start.3) | async-done | bytes 704544 | tf_op jit(solution)/shard_map/all_to_all | solution.py:84
  386.0 2.0 scatter_fusion.1
  394.1 88.2 %all-reduce.3.cloned.1.call-done = (f32[128,256]{1,0:T(8,128)}, f32[256,172]{0,1:T(8,128)}) async-done(((f32[128,256]{1,0:T(8,128)}, f32[256,172]{0,1:T(8,128)}), (f32[128,256]{1,0:T(8,128)}, f32[256,172]{0,1:T(8,128)})) %all-reduce.3.cloned.1.call-update) | async-done | bytes 307216 | tf_op jit(solution)/shard_map/psum | solution.py:94
  482.2 1.6 copy.78
  483.8 1.6 copy.79
  (168 shorter events, 90.5 us)
Async XLA Ops:
  7.2 73.4 %copy-start = (bf16[256,172]{0,1:T(8,128)(2,1)S(1)}, bf16[256,172]{0,1:T(8,128)(2,1)}, u32[]{:S(2)}) copy-start(bf16[256,172]{0,1:T(8,128)(2,1)} %param.19) | copy-start | bytes 264196
  21.9 6.0 %copy-start.8 = (s32[16]{0:T(128)}, s32[16]{0:T(128)S(1)}, u32[]{:S(2)}) copy-start(s32[16]{0:T(128)S(1)} %reduce.2) | copy-start | bytes 196
  24.3 18.0 %all-to-all-start.1 = ((bf16[16,128,128]{2,1,0:T(8,128)(2,1)}), bf16[16,128,128]{2,1,0:T(8,128)(2,1)S(1)}, u32[]{:S(2)}, u32[]{:S(2)}) async-start(bf16[16,128,128]{2,1,0:T(8,128)(2,1)} %gather_fusion.2), calls=%async_computation.1 | async-start | bytes 1048576 | tf_op jit(solution)/shard_map/all_to_all | solution.py:58
  27.9 14.4 %copy-start.4 = (bf16[768,128]{1,0:T(8,128)(2,1)S(1)}, bf16[768,128]{1,0:T(8,128)(2,1)}, u32[]{:S(2)}) copy-start(bf16[768,128]{1,0:T(8,128)(2,1)} %param.13) | copy-start | bytes 589828
  42.4 37.1 %copy-start.7 = (bf16[128,256]{1,0:T(8,128)(2,1)S(1)}, bf16[128,256]{1,0:T(8,128)(2,1)}, u32[]{:S(2)}) copy-start(bf16[128,256]{1,0:T(8,128)(2,1)} %param.18) | copy-start | bytes 196612
  79.4 1.7 copy-start.5
  79.7 0.9 copy-start.2
  82.6 21.7 %all-to-all-start.2 = ((bf16[16,128,172]{1,2,0:T(8,128)(2,1)}), bf16[16,128,172]{1,2,0:T(8,128)(2,1)S(1)}, u32[]{:S(2)}, u32[]{:S(2)}) async-start(bf16[16,128,172]{1,2,0:T(8,128)(2,1)} %gather_fusion.3), calls=%async_computation.2 | async-start | bytes 1441792 | tf_op jit(solution)/shard_map/all_to_all | solution.py:65
  108.0 94.1 %copy-start.10 = (s32[768]{0:T(1024)S(1)}, s32[768]{0:T(1024)}, u32[]{:S(2)}) copy-start(s32[768]{0:T(1024)} %param.17) | copy-start | bytes 9220
  114.5 4.3 copy-start.1
  130.1 4.3 copy-start.1
  145.7 4.3 copy-start.1
  161.4 4.3 copy-start.1
  177.0 4.3 copy-start.1
  192.6 4.3 copy-start.1
  361.9 22.9 %all-to-all-start.3 = ((bf16[16,128,172]{1,2,0:T(8,128)(2,1)}), bf16[16,128,172]{1,2,0:T(8,128)(2,1)}, u32[]{:S(2)}, u32[]{:S(2)}) async-start(bf16[16,128,172]{1,2,0:T(8,128)(2,1)} %slice.19), calls=%async_computation.3 | async-start | bytes 1441792 | tf_op jit(solution)/shard_map/all_to_all | solution.py:84
  367.1 18.9 %copy-start.9 = (s32[16]{0:T(128)S(1)}, s32[16]{0:T(128)}, u32[]{:S(2)}) copy-start(s32[16]{0:T(128)} %copy-done.8) | copy-start | bytes 196
  367.1 115.1 %all-reduce.3.cloned.1.call-start = ((), (), s32[]{:S(2)}) async-start(), calls=%async_computation.4 | async-start | bytes 622592 | tf_op jit(solution)/shard_map/psum | solution.py:94
  388.2 1.1 copy-start.3
  390.8 0.9 copy-start.6
Sparse Core Ops, SparseCore 0:
  393.0 89.1 all-reduce.2
where the time goes:
time: 497 us; the launch traced here: 492 us
  local copies, waits for them, and re-layouts  159 us (32%)
  waiting for transfers between devices  125 us (25%)
  other arithmetic  93.5 us (19%)
  matrix products  39.1 us (8%)
  loops' own time  34.1 us (7%)
  between operations  14.4 us (3%)
  blocking collectives  13.6 us (3%)
  starting transfers between devices  13 us (3%)
    psum x1, waiting for transfers between devices, local(): grad_one = lax.psum(grad_one_local, 'dom')  88.2 us
    reshape x12, local copies, waits for them, and re-layouts, back_row(): dot_right(tile.T, grad_blocks[index]).reshape(kr_count, block_size, classes)  61.4 us
    scatter-add x6, other arithmetic, back_row(): return (carry.at[block_cols[index]].add(terms), None)  45.8 us
    gather x12, local copies, waits for them, and re-layouts, one_row(): taken = table[block_cols[index]].reshape(kr_count * block_size, width)  25.6 us
    dot_general x14, matrix products, dot_right(): jnp.dot(left, low, preferred_element_type=jnp.float32)  22.9 us
    another operation x2, loops' own time, aggregate_rows(): rows = lax.map(one_row, jnp.arange(count, dtype=jnp.int32))  22.2 us
    convert_element_type x7, other arithmetic, split_parts(): high = lax.optimization_barrier(value.astype(jnp.bfloat16))  18.4 us
    all_to_all x1, waiting for transfers between devices, local(): lax.all_to_all(product_blocks[wanted].astype(jnp.bfloat16), 'dom', split_...  17.6 us
  transfers between devices with their start and end apart: 4, of which 4 were waited for; matrix products, arithmetic and copies ran while one was open for 3% of the time, Pallas kernels for 0%

commit v1 on v0

v1 whole, which is shorter than its diff:
```python
import functools
import math

import jax
import jax.numpy as jnp
from jax import lax
from jax.experimental import pallas as pl
from jax.experimental.pallas import tpu as pltpu
from jax.sharding import PartitionSpec as P

F32 = jnp.float32
BF16 = jnp.bfloat16
NT = (((1,), (1,)), ((), ()))


def dot(left, right):
    return jnp.dot(left, right, preferred_element_type=F32)


def dot_nt(left, right):
    return lax.dot_general(left, right, NT, preferred_element_type=F32)


def split_rows(value):
    high = value.astype(BF16)
    low = (value - high.astype(F32)).astype(BF16)
    return jnp.concatenate([high, low], axis=0)


def fold_rows(value, rows):
    return value[:rows] + value[rows:]


def merge_kernel(table, kr, cols_ref, tiles_ref, out_ref, acc):
    row = pl.program_id(0)
    bs = tiles_ref.shape[2]

    def clear(c, _):
        acc[c] = jnp.zeros((bs, bs), F32)
        return 0

    lax.fori_loop(0, table, clear, 0, unroll=2)

    def add(k, _):
        c = cols_ref[row, k]
        acc[c] += tiles_ref[0, k].astype(F32)
        return 0

    lax.fori_loop(0, kr, add, 0, unroll=4)

    def put(c, _):
        out_ref[:, pl.ds(pl.multiple_of(c * bs, bs), bs)] = acc[c].astype(BF16)
        return 0

    lax.fori_loop(0, table, put, 0, unroll=2)


def merge(tiles, cols, table):
    count, kr, bs, _ = tiles.shape
    return pl.pallas_call(
        functools.partial(merge_kernel, table, kr),
        out_shape=jax.ShapeDtypeStruct((count * bs, table * bs), BF16),
        grid_spec=pltpu.PrefetchScalarGridSpec(
            num_scalar_prefetch=1,
            grid=(count,),
            in_specs=[pl.BlockSpec((1, kr, bs, bs), lambda i, c: (i, 0, 0, 0))],
            out_specs=pl.BlockSpec((bs, table * bs), lambda i, c: (i, 0)),
            scratch_shapes=[pltpu.VMEM((table, bs, bs), F32)],
        ),
        compiler_params=pltpu.CompilerParams(vmem_limit_bytes=48 * 1024 * 1024),
        name="merge_tiles",
    )(cols, tiles)


def main_kernel(
    parts, count, bs, classes, cp, rp, nodes,
    req_ref, cols_ref, tiles_hbm, feat_ref, adj_ref, lab_ref, w1t_ref, w2t_ref, w2w_ref,
    logits_ref, one_ref, two_ref,
    idx_out, idx_in, stage, feat_in, prod_in, back_in, grads, grads_in, final,
    tiles, agg, hid, gate, prod, parts_hl, own_acc,
    tile_sem, send_sem, idx_sem, feat_sem, prod_sem, back_sem, rs_sem, ag_sem,
):
    grp = lax.axis_index("grp")
    me = lax.axis_index("dom")
    chips = parts // 2
    kr = tiles.shape[1]
    my_chip = me // 2
    own = count * bs

    def peer_at(s):
        return lax.rem(me + s, parts)

    def send(src, dst, sem, peer):
        return pltpu.make_async_remote_copy(
            src_ref=src, dst_ref=dst, send_sem=send_sem.at[peer], recv_sem=sem.at[me],
            device_id=(grp, peer), device_id_type=pl.DeviceIdType.MESH,
        )

    def arrival(buffer, sem, peer):
        return pltpu.make_async_remote_copy(
            src_ref=buffer, dst_ref=buffer, send_sem=send_sem.at[peer], recv_sem=sem.at[peer],
            device_id=(grp, peer), device_id_type=pl.DeviceIdType.MESH,
        )

    def each_peer(body):
        def step(s, _):
            body(peer_at(s))
            return 0

        lax.fori_loop(1, parts, step, 0)

    def each_chip(body):
        def step(s, _):
            body(lax.rem(my_chip + s, chips))
            return 0

        lax.fori_loop(0, chips, step, 0)

    def landed(buffer, sem, peer):
        @pl.when(peer != me)
        def _():
            arrival(buffer, sem, peer).wait_recv()

    def tile_copy(row):
        return pltpu.make_async_copy(tiles_hbm.at[row], tiles.at[row], tile_sem.at[row])

    for row in range(count):
        tile_copy(row).start()

    barrier = pltpu.get_barrier_semaphore()
    each_peer(lambda peer: pl.semaphore_signal(
        barrier, inc=1, device_id=(grp, peer), device_id_type=pl.DeviceIdType.MESH))
    pl.semaphore_wait(barrier, parts - 1)

    def ask(s, _):
        peer = peer_at(s)
        idx_out[peer] = jnp.full((8, 128), req_ref[0, peer], jnp.int32)
        send(idx_out.at[peer], idx_in.at[me], idx_sem, peer).start()
        return 0

    lax.fori_loop(1, parts, ask, 0)
    idx_in[me] = jnp.full((8, 128), req_ref[0, me], jnp.int32)

    def pick(peer, blocks):
        wanted = jnp.broadcast_to(idx_in[peer][:1], blocks[0].shape)
        out = blocks[0]
        for b in range(1, count):
            out = jnp.where(wanted == b, blocks[b], out)
        return out

    each_peer(lambda peer: send(idx_out.at[peer], idx_in.at[me], idx_sem, peer).wait_send())

    def send_features(peer):
        arrival(idx_in.at[peer], idx_sem, peer).wait_recv()
        blocks = [feat_ref[b * bs:(b + 1) * bs, :].astype(F32) for b in range(count)]
        stage[peer, 0:bs, :] = pick(peer, blocks).astype(BF16)
        send(stage.at[peer, 0:bs, :], feat_in.at[count + me], feat_sem, peer).start()

    each_peer(send_features)
    blocks = [feat_ref[b * bs:(b + 1) * bs, :].astype(F32) for b in range(count)]
    feat_in[count + me] = pick(me, blocks).astype(BF16)
    for b in range(count):
        feat_in[b] = feat_ref[b * bs:(b + 1) * bs, :]

    each_peer(lambda peer: arrival(feat_in.at[count + peer], feat_sem, peer).wait_recv())

    def aggregate_row(row, _):
        tile_copy(row).wait()
        total = jnp.zeros((bs, feat_ref.shape[1]), F32)
        for k in range(0, kr, 2):
            pair = jnp.concatenate(
                [feat_in[cols_ref[row, k]], feat_in[cols_ref[row, k + 1]]], axis=0)
            total += dot(jnp.concatenate([tiles[row, k], tiles[row, k + 1]], axis=1), pair)
        agg[pl.ds(pl.multiple_of(row * bs, bs), bs), :] = total.astype(BF16)
        return 0

    lax.fori_loop(0, count, aggregate_row, 0)
    each_peer(lambda peer: send(
        stage.at[peer, 0:bs, :], feat_in.at[count + me], feat_sem, peer).wait_send())

    pre = dot_nt(w1t_ref[...], agg[...])
    gate[...] = jnp.where(pre > 0.0, 1.0, 0.0).astype(F32)
    hid[...] = jnp.maximum(pre, 0.0).astype(BF16)
    prod[...] = dot(w2t_ref[...], hid[...])

    def product_block(peer):
        return pick(peer, [prod[:, b * bs:(b + 1) * bs] for b in range(count)]).astype(BF16)

    def send_product(peer):
        stage[peer] = product_block(peer)
        send(stage.at[peer], prod_in.at[me], prod_sem, peer).start()

    each_peer(send_product)
    prod_in[me] = product_block(me)

    parts_hl[...] = split_rows(prod[...])
    own_acc[...] = fold_rows(dot_nt(parts_hl[...], adj_ref[:, 0:own]), cp)

    def add_product(chip):
        landed(prod_in.at[2 * chip], prod_sem, 2 * chip)
        landed(prod_in.at[2 * chip + 1], prod_sem, 2 * chip + 1)
        pair = jnp.concatenate([prod_in[2 * chip], prod_in[2 * chip + 1]], axis=1)
        cols = adj_ref[:, pl.ds(pl.multiple_of(own + chip * 2 * bs, 128), 2 * bs)]
        own_acc[...] += dot_nt(pair, cols)

    each_chip(add_product)
    each_peer(lambda peer: send(stage.at[peer], prod_in.at[me], prod_sem, peer).wait_send())

    logits = own_acc[...]
    logits_ref[...] = logits[:classes]
    rows = lax.broadcasted_iota(jnp.int32, (cp, own), 0)
    real = rows < classes
    top = jnp.max(jnp.where(real, logits, -jnp.inf), axis=0, keepdims=True)
    expo = jnp.where(real, jnp.exp(logits - top), 0.0)
    probs = expo / jnp.sum(expo, axis=0, keepdims=True)
    onehot = jnp.where(rows == lab_ref[...], 1.0, 0.0)
    parts_hl[...] = split_rows((probs - onehot) / math.sqrt(nodes))

    def send_back(chip):
        cols = adj_ref[:, pl.ds(pl.multiple_of(own + chip * 2 * bs, 128), 2 * bs)]
        pair = fold_rows(dot(parts_hl[...], cols), cp).astype(BF16)
        for core in range(2):
            peer = 2 * chip + core
            block = pair[:, core * bs:(core + 1) * bs]

            @pl.when(peer != me)
            def _():
                stage[peer] = block
                send(stage.at[peer], back_in.at[me], back_sem, peer).start()

            @pl.when(peer == me)
            def _():
                back_in[peer] = block

    each_chip(send_back)
    own_acc[...] = fold_rows(dot(parts_hl[...], adj_ref[:, 0:own]), cp)

    def add_back(chip):
        for core in range(2):
            peer = 2 * chip + core
            landed(back_in.at[peer], back_sem, peer)
            block = back_in[peer].astype(F32)
            wanted = jnp.broadcast_to(idx_in[peer][:1], (cp, bs))
            for b in range(count):
                own_acc[:, b * bs:(b + 1) * bs] += jnp.where(wanted == b, block, 0.0)

    each_chip(add_back)
    each_peer(lambda peer: send(stage.at[peer], back_in.at[me], back_sem, peer).wait_send())

    split = split_rows(own_acc[...])
    parts_hl[...] = split
    two = fold_rows(dot_nt(split, hid[...]), cp)
    grad_pre = dot(w2w_ref[...], parts_hl[...]) * gate[...]
    one = fold_rows(dot(split_rows(grad_pre), agg[...]), hid.shape[0])
    hidden = hid.shape[0]
    halves = hidden // 128
    used = halves * cp + hidden
    for h in range(halves):
        grads[h * cp:(h + 1) * cp, :] = two[:, h * 128:(h + 1) * 128]
    grads[halves * cp:used, :] = one
    if used < parts * rp:
        grads[used:, :] = jnp.zeros((parts * rp - used, 128), F32)

    def share(peer):
        return pl.ds(pl.multiple_of(peer * rp, 8), rp)

    each_peer(lambda peer: send(
        grads.at[share(peer)], grads_in.at[me], rs_sem, peer).start())
    grads_in[me] = grads[share(me)]

    def take(peer):
        arrival(grads_in.at[peer], rs_sem, peer).wait_recv()

    each_peer(take)
    each_peer(lambda peer: send(
        grads.at[share(peer)], grads_in.at[me], rs_sem, peer).wait_send())
    total = lax.fori_loop(0, parts, lambda p, t: t + grads_in[p], jnp.zeros((rp, 128), F32))
    final[share(me)] = total
    each_peer(lambda peer: send(
        final.at[share(me)], final.at[share(me)], ag_sem, peer).start())

    def take_total(peer):
        arrival(final.at[share(peer)], ag_sem, peer).wait_recv()

    each_peer(take_total)
    each_peer(lambda peer: send(
        final.at[share(me)], final.at[share(me)], ag_sem, peer).wait_send())
    for h in range(halves):
        two_ref[:, h * 128:(h + 1) * 128] = final[h * cp:h * cp + classes, :]
    one_ref[...] = final[halves * cp:used, :].T


def local(features, block_tiles, block_cols, halo_request, labels, weight_one, weight_two):
    parts = lax.axis_size("dom")
    count, bs, kr, _ = block_tiles.shape
    width = features.shape[1]
    hidden, classes = weight_two.shape
    cp = -(-classes // 16) * 16
    own = count * bs
    table = count + parts
    used = (hidden // 128) * cp + hidden
    rp = -(-used // (8 * parts)) * 8
    tiles = block_tiles.transpose(0, 2, 1, 3)
    adj = merge(tiles, block_cols, table)
    w2t = jnp.pad(weight_two.T, ((0, cp - classes), (0, 0)))
    w2w = jnp.pad(weight_two, ((0, 0), (0, cp - classes)))
    w2w = jnp.concatenate([w2w, w2w], axis=1)
    vmem = pl.BlockSpec(memory_space=pltpu.VMEM)
    smem = pl.BlockSpec(memory_space=pltpu.SMEM)
    dma = pltpu.SemaphoreType.DMA((parts,))
    logits, one, two = pl.pallas_call(
        functools.partial(main_kernel, parts, count, bs, classes, cp, rp, parts * own),
        out_shape=(
            jax.ShapeDtypeStruct((classes, own), F32),
            jax.ShapeDtypeStruct((width, hidden), F32),
            jax.ShapeDtypeStruct((classes, hidden), F32),
        ),
        in_specs=[smem, smem, pl.BlockSpec(memory_space=pl.ANY)] + [vmem] * 6,
        out_specs=(vmem, vmem, vmem),
        scratch_shapes=[
            pltpu.VMEM((parts, 8, 128), jnp.int32),
            pltpu.VMEM((parts, 8, 128), jnp.int32),
            pltpu.VMEM((parts, cp, bs), BF16),
            pltpu.VMEM((table, bs, width), BF16),
            pltpu.VMEM((parts, cp, bs), BF16),
            pltpu.VMEM((parts, cp, bs), BF16),
            pltpu.VMEM((parts * rp, 128), F32),
            pltpu.VMEM((parts, rp, 128), F32),
            pltpu.VMEM((parts * rp, 128), F32),
            pltpu.VMEM((count, kr, bs, bs), BF16),
            pltpu.VMEM((own, width), BF16),
            pltpu.VMEM((hidden, own), BF16),
            pltpu.VMEM((hidden, own), F32),
            pltpu.VMEM((cp, own), F32),
            pltpu.VMEM((2 * cp, own), BF16),
            pltpu.VMEM((cp, own), F32),
            pltpu.SemaphoreType.DMA((count,)),
            dma, dma, dma, dma, dma, dma, dma,
        ],
        compiler_params=pltpu.CompilerParams(
            collective_id=0, has_side_effects=True, vmem_limit_bytes=63 * 1024 * 1024),
        name="graph_layers",
    )(halo_request, block_cols, tiles, features, adj, labels.reshape(1, own), weight_one.T, w2t, w2w)
    return (logits.T, one, two.T)


def solution(mesh):
    placed = (
        P(("grp", "dom"), None),
        P(("grp", "dom"), None, None, None),
        P(("grp", "dom"), None),
        P(("grp", "dom"), None),
        P(("grp", "dom")),
        P(),
        P(),
    )
    return jax.shard_map(
        local,
        mesh=mesh,
        in_specs=placed,
        out_specs=(P(("grp", "dom"), None), P("grp", None), P("grp", None)),
        check_vma=False,
    )
```

time: 497 us -> 105 us (0.21)
  local copies, waits for them, and re-layouts: 159 us -> 13.1 us
  waiting for transfers between devices: 125 us -> 0 us
  other arithmetic: 93.5 us -> 0.79 us
  Pallas kernels: 0 us -> 90.4 us
  matrix products: 39.1 us -> 0 us
  loops' own time: 34.1 us -> 0 us
  between operations: 14.4 us -> 0.67 us
  blocking collectives: 13.6 us -> 0 us
  starting transfers between devices: 13 us -> 0 us
    pallas_call x0 -> x2, Pallas kernels: none -> 90.4 us  [the longest x1 82.9 us: local(): pl.pallas_call(functools.partial(main_kernel, parts, count, bs, classes,...]
    psum x1 -> x0, waiting for transfers between devices: 88.2 us -> none  [local(): grad_one = lax.psum(grad_one_local, 'dom')]
    reshape x14 -> x1, local copies, waits for them, and re-layouts: 61.6 us -> 1.27 us  [local(): labels.reshape(1, own)]
    scatter-add x7 -> x0, other arithmetic: 47.8 us -> none  [the longest x6 45.8 us: back_row(): return (carry.at[block_cols[index]].add(terms), None)]
    dot_general x38 -> x0, matrix products: 39.1 us -> none  [the longest x14 22.9 us: dot_right(): jnp.dot(left, low, preferred_element_type=jnp.float32)]
    all_to_all x3 -> x0, waiting for transfers between devices: 37 us -> none  [the longest x1 17.6 us: local(): lax.all_to_all(product_blocks[wanted].astype(jnp.bfloat16), 'dom', split_...]
    dynamic_slice x36 -> x0, local copies, waits for them, and re-layouts: 36.8 us -> none  [the longest x12 17.6 us: one_row(): tile = block_tiles[index].reshape(block_size, kr_count * block_size)]
    another operation x3 -> x0, loops' own time: 34.1 us -> none  [the longest x2 22.2 us: aggregate_rows(): rows = lax.map(one_row, jnp.arange(count, dtype=jnp.int32))]
  transfers between devices with their start and end apart: 4 -> 0, of which waited for: 4 -> 0; matrix products, arithmetic and copies ran while one was open for 3% -> 0% of each run, Pallas kernels for 0% -> 0%
where the time goes in v1:
time: 105 us
  Pallas kernels  90.4 us (86%)
  local copies, waits for them, and re-layouts  13.1 us (12%)
    pallas_call x1, Pallas kernels, local(): pl.pallas_call(functools.partial(main_kernel, parts, count, bs, classes,...  82.9 us
    unnamed x9, local copies, waits for them, and re-layouts  10.3 us
    pallas_call x1, Pallas kernels, merge(): pl.pallas_call(functools.partial(merge_kernel, table, kr), out_shape=jax....  7.55 us

profile of v1, /device:TPU:0, one launch (start us, length us, event | category | flops | bytes accessed | tf_op | source)
XLA Modules:
  0.0 105.0 jit_solution(14186846737792748663)
XLA Ops:
  0.6 1.3 %reshape.9.lab_ref = s32[1,768]{1,0:T(1,128)} reshape(s32[768]{0:T(1024)} %param.11) | data formatting | bytes 6144 | tf_op jit(solution)/shard_map/reshape | solution.py:343
  1.9 1.6 %copy.10 = bf16[128,256]{0,1:T(8,128)(2,1)} copy(bf16[128,256]{1,0:T(8,128)(2,1)} %param.12) | data formatting | bytes 131072 | tf_op args[5]
  3.5 1.5 %pad.8.w2t_ref = bf16[176,256]{1,0:T(8,128)(2,1)} pad(bf16[172,256]{1,0:T(8,128)(2,1)} %bitcast.8, bf16[]{:T(256)} %constant.2.clone.1), padding=0_4x0_0 | pad | bytes 178178 | tf_op jit(solution)/shard_map/jit(_pad)/pad | solution.py:305
  5.0 1.0 copy.11
  6.0 0.8 pad_maximum_fusion.w2w_ref
  6.8 0.0 copy-start.1
  6.8 0.7 copy-done.1
  7.5 7.5 %merge_tiles.1.adj_ref = bf16[768,2816]{1,0:T(8,128)(2,1)S(1)} custom-call(s32[6,44]{1,0:T(8,128)S(1)} %copy-done.1, bf16[6,44,128,128]{3,2,1,0:T(8,128)(2,1)} %bitcast.5), custom_call_target="tpu_custom_call" | custom-call | tf_op jit(solution)/shard_map/merge_tiles/pallas_call | solution.py:60
  15.1 0.0 copy-start
  15.1 2.0 %copy-done = bf16[768,2816]{1,0:T(8,128)(2,1)} copy-done((bf16[768,2816]{1,0:T(8,128)(2,1)}, bf16[768,2816]{1,0:T(8,128)(2,1)S(1)}, u32[]{:S(2)}) %copy-start) | copy-done | bytes 4325400
  17.0 82.9 %graph_layers.1 = (f32[172,768]{1,0:T(8,128)}, f32[128,256]{1,0:T(8,128)}, f32[172,256]{1,0:T(8,128)}) custom-call(s32[1,16]{1,0:T(1,128)} %req_ref.1, s32[6,44]{1,0:T(8,128)} %cols_ref.3, bf16[6,44,128,128]{3,2,1,0:T(8,128)(2,1)} %bitcast.6, bf16[768,128]{1,0:T(8,128)(2,1)} %feat_ref.1, bf16[768,2816]{1,0:T(8,128)(2,1)} %copy-done, ...), custom_call_target="tpu_custom_call" | custom-call | tf_op jit(solution)/shard_map/graph_layers/pallas_call | solution.py:311
  99.9 1.9 %copy.15 = f32[768,172]{0,1:T(8,128)} copy(f32[768,172]{0,1:T(8,128)} %bitcast.7) | data formatting | bytes 1056768
  101.8 1.6 %copy.16 = f32[128,256]{1,0:T(8,128)} copy(f32[128,256]{1,0:T(8,128)} %get-tuple-element.13) | data formatting | bytes 262144
  103.4 1.6 %copy.17 = f32[256,172]{0,1:T(8,128)} copy(f32[256,172]{0,1:T(8,128)} %bitcast.10) | data formatting | bytes 352256
  (1 shorter events, 0.0 us)
Async XLA Ops:
  6.8 0.7 copy-start.1
  15.1 2.0 %copy-start = (bf16[768,2816]{1,0:T(8,128)(2,1)}, bf16[768,2816]{1,0:T(8,128)(2,1)S(1)}, u32[]{:S(2)}) copy-start(bf16[768,2816]{1,0:T(8,128)(2,1)S(1)} %merge_tiles.1.adj_ref) | copy-start | bytes 12976132

commit v2 on v1

v2 whole, which is shorter than its diff:
```python
import functools
import math

import jax
import jax.numpy as jnp
from jax import lax
from jax.experimental import pallas as pl
from jax.experimental.pallas import tpu as pltpu
from jax.sharding import PartitionSpec as P

F32 = jnp.float32
BF16 = jnp.bfloat16
NT = (((1,), (1,)), ((), ()))


def dot(left, right):
    return jnp.dot(left, right, preferred_element_type=F32)


def dot_nt(left, right):
    return lax.dot_general(left, right, NT, preferred_element_type=F32)


def split_rows(value):
    high = value.astype(BF16)
    low = (value - high.astype(F32)).astype(BF16)
    return jnp.concatenate([high, low], axis=0)


def fold_rows(value, rows):
    return value[:rows] + value[rows:]


def main_kernel(
    parts, count, kr, bs, classes, cp, rp, nodes,
    req_ref, cols_ref, prev_ref, last_ref, tiles_hbm, feat_ref, lab_ref, w1_ref, w2t_ref,
    logits_ref, sums_ref,
    idx_out, idx_in, stage, feat_tab, agg_tab, tiles, chain, adj,
    grads, grads_in, final, w1t, w2pad, w2t, w2, acc, g_hl, two_acc, one_acc,
    tile_sem, send_sem, idx_sem, feat_sem, agg_sem, rs_sem, ag_sem,
):
    grp = lax.axis_index("grp")
    me = lax.axis_index("dom")
    chips = parts // 2
    my_chip = me // 2
    own_pairs = count // 2
    table = count + parts
    own = count * bs
    hidden = w1_ref.shape[1]
    halves = hidden // 128
    used = halves * cp + hidden

    def peer_at(s):
        return lax.rem(me + s, parts)

    def send(src, dst, sem, peer):
        return pltpu.make_async_remote_copy(
            src_ref=src, dst_ref=dst, send_sem=send_sem.at[peer], recv_sem=sem.at[me],
            device_id=(grp, peer), device_id_type=pl.DeviceIdType.MESH,
        )

    def arrival(buffer, sem, peer):
        return pltpu.make_async_remote_copy(
            src_ref=buffer, dst_ref=buffer, send_sem=send_sem.at[peer], recv_sem=sem.at[peer],
            device_id=(grp, peer), device_id_type=pl.DeviceIdType.MESH,
        )

    def each_peer(body):
        def step(s, _):
            body(peer_at(s))
            return 0

        lax.fori_loop(1, parts, step, 0)

    def tile_copy(row):
        return pltpu.make_async_copy(tiles_hbm.at[row], tiles.at[row], tile_sem.at[row])

    for row in range(count):
        tile_copy(row).start()

    barrier = pltpu.get_barrier_semaphore()
    each_peer(lambda peer: pl.semaphore_signal(
        barrier, inc=1, device_id=(grp, peer), device_id_type=pl.DeviceIdType.MESH))
    pl.semaphore_wait(barrier, parts - 1)

    def ask(s, _):
        peer = peer_at(s)
        idx_out[peer] = jnp.full((8, 128), req_ref[0, peer], jnp.int32)
        send(idx_out.at[peer], idx_in.at[me], idx_sem, peer).start()
        return 0

    lax.fori_loop(1, parts, ask, 0)
    idx_in[me] = jnp.full((8, 128), req_ref[0, me], jnp.int32)
    w1t[...] = w1_ref[...].astype(F32).T.astype(BF16)
    w2pad[...] = jnp.zeros(w2pad.shape, F32)
    w2pad[0:classes, :] = w2t_ref[...].astype(F32)
    w2t[...] = w2pad[0:cp, :].astype(BF16)
    w2[...] = w2pad[...].T[:, 0:cp].astype(BF16)
    for b in range(count):
        feat_tab[b] = feat_ref[b * bs:(b + 1) * bs, :]
    each_peer(lambda peer: send(idx_out.at[peer], idx_in.at[me], idx_sem, peer).wait_send())

    def pick(peer, tab):
        wanted = jnp.broadcast_to(idx_in[peer][:1], tab.shape[1:])
        out = tab[0].astype(F32)
        for b in range(1, count):
            out = jnp.where(wanted == b, tab[b].astype(F32), out)
        return out.astype(BF16)

    def exchange(tab, sem, first):
        def go(peer):
            if first:
                arrival(idx_in.at[peer], idx_sem, peer).wait_recv()
            stage[peer] = pick(peer, tab)
            send(stage.at[peer], tab.at[count + me], sem, peer).start()

        each_peer(go)
        tab[count + me] = pick(me, tab)

    def sent(tab, sem):
        each_peer(lambda peer: send(stage.at[peer], tab.at[count + me], sem, peer).wait_send())

    exchange(feat_tab, feat_sem, True)

    chain[0] = jnp.zeros((bs, bs), F32)

    def merge_row(row, _):
        tile_copy(row).wait()

        def add(k, _):
            chain[k + 1] = tiles[row, k].astype(F32) + chain[prev_ref[row, k]]
            return 0

        lax.fori_loop(0, kr, add, 0, unroll=4)
        rows = pl.ds(pl.multiple_of(row * bs, bs), bs)

        def put(c, _):
            adj[rows, pl.ds(pl.multiple_of(c * bs, bs), bs)] = chain[last_ref[row, c]].astype(BF16)
            return 0

        lax.fori_loop(0, table, put, 0, unroll=2)
        return 0

    lax.fori_loop(0, count, merge_row, 0)

    each_peer(lambda peer: arrival(feat_tab.at[count + peer], feat_sem, peer).wait_recv())

    def aggregate_row(row, _):
        total = jnp.zeros((bs, feat_ref.shape[1]), F32)
        for k in range(0, kr, 2):
            pair = jnp.concatenate(
                [feat_tab[cols_ref[row, k]], feat_tab[cols_ref[row, k + 1]]], axis=0)
            total += dot(jnp.concatenate([tiles[row, k], tiles[row, k + 1]], axis=1), pair)
        agg_tab[row] = total.astype(BF16)
        return 0

    lax.fori_loop(0, count, aggregate_row, 0)
    sent(feat_tab, feat_sem)

    exchange(agg_tab, agg_sem, False)

    def pair_cols(j):
        return adj[:, pl.ds(pl.multiple_of(j * 2 * bs, 2 * bs), 2 * bs)]

    def pair_agg(j):
        return agg_tab[pl.ds(2 * j, 2)].reshape(2 * bs, w1_ref.shape[0])

    def forward(j):
        pre = dot_nt(w1t[...], pair_agg(j))
        prod = dot(w2t[...], jnp.maximum(pre, 0.0).astype(BF16))
        return fold_rows(dot_nt(split_rows(prod), pair_cols(j)), cp)

    acc[...] = forward(0)
    for j in range(1, own_pairs):
        acc[...] += forward(j)

    def halo(s, _):
        chip = lax.rem(my_chip + s, chips)
        for core in range(2):
            peer = 2 * chip + core

            @pl.when(peer != me)
            def _():
                arrival(agg_tab.at[count + peer], agg_sem, peer).wait_recv()

        acc[...] += forward(own_pairs + chip)
        return 0

    lax.fori_loop(0, chips, halo, 0)
    sent(agg_tab, agg_sem)

    logits = acc[...]
    logits_ref[...] = logits
    rows = lax.broadcasted_iota(jnp.int32, (cp, own), 0)
    real = rows < classes
    top = jnp.max(jnp.where(real, logits, -jnp.inf), axis=0, keepdims=True)
    expo = jnp.where(real, jnp.exp(logits - top), 0.0)
    probs = expo / jnp.sum(expo, axis=0, keepdims=True)
    labels = jnp.concatenate([lab_ref[b:b + 1, :] for b in range(count)], axis=1)
    onehot = jnp.where(rows == labels, 1.0, 0.0)
    g_hl[...] = split_rows((probs - onehot) / math.sqrt(nodes))

    two_acc[...] = jnp.zeros(two_acc.shape, F32)
    one_acc[...] = jnp.zeros(one_acc.shape, F32)

    def backward(j, _):
        agg = pair_agg(j)
        pre = dot_nt(w1t[...], agg)
        term = split_rows(fold_rows(dot(g_hl[...], pair_cols(j)), cp))
        two_acc[...] += fold_rows(dot_nt(term, jnp.maximum(pre, 0.0).astype(BF16)), cp)
        grad_hidden = dot(w2[...], term[:cp]) + dot(w2[...], term[cp:])
        grad_pre = jnp.where(pre > 0.0, grad_hidden, 0.0)
        one_acc[...] += fold_rows(dot(split_rows(grad_pre), agg), hidden)
        return 0

    lax.fori_loop(0, table // 2, backward, 0, unroll=table <= 32)

    for h in range(halves):
        grads[h * cp:(h + 1) * cp, :] = two_acc[:, h * 128:(h + 1) * 128]
    grads[halves * cp:used, :] = one_acc[...]
    if used < parts * rp:
        grads[used:, :] = jnp.zeros((parts * rp - used, 128), F32)

    def share(peer):
        return pl.ds(pl.multiple_of(peer * rp, 8), rp)

    each_peer(lambda peer: send(
        grads.at[share(peer)], grads_in.at[me], rs_sem, peer).start())
    grads_in[me] = grads[share(me)]

    def take(peer):
        arrival(grads_in.at[peer], rs_sem, peer).wait_recv()

    each_peer(take)
    each_peer(lambda peer: send(
        grads.at[share(peer)], grads_in.at[me], rs_sem, peer).wait_send())
    total = lax.fori_loop(0, parts, lambda p, t: t + grads_in[p], jnp.zeros((rp, 128), F32))
    final[share(me)] = total
    each_peer(lambda peer: send(
        final.at[share(me)], final.at[share(me)], ag_sem, peer).start())

    def take_total(peer):
        arrival(final.at[share(peer)], ag_sem, peer).wait_recv()

    each_peer(take_total)
    each_peer(lambda peer: send(
        final.at[share(me)], final.at[share(me)], ag_sem, peer).wait_send())
    sums_ref[...] = final[0:used, :]


def place_kernel(classes, cp, hidden, logits_ref, sums_ref, out_ref, one_ref, two_ref):
    halves = hidden // 128
    out_ref[...] = logits_ref[0:classes, :]
    for h in range(halves):
        two_ref[:, h * 128:(h + 1) * 128] = sums_ref[h * cp:h * cp + classes, :]
    one_ref[...] = sums_ref[halves * cp:, :].T


def local(features, block_tiles, block_cols, halo_request, labels, weight_one, weight_two):
    parts = lax.axis_size("dom")
    count, bs, kr, _ = block_tiles.shape
    width = features.shape[1]
    hidden, classes = weight_two.shape
    cp = -(-classes // 16) * 16
    cw = -(-classes // 128) * 128
    own = count * bs
    table = count + parts
    used = (hidden // 128) * cp + hidden
    rp = -(-used // (8 * parts)) * 8
    tiles = block_tiles.transpose(0, 2, 1, 3)
    slot = jnp.arange(kr, dtype=jnp.int32)
    same = block_cols[:, :, None] == block_cols[:, None, :]
    before = slot[None, None, :] < slot[None, :, None]
    prev = jnp.max(jnp.where(same & before, slot[None, None, :] + 1, 0), axis=2)
    here = block_cols[:, None, :] == jnp.arange(table, dtype=jnp.int32)[None, :, None]
    last = jnp.max(jnp.where(here, slot[None, None, :] + 1, 0), axis=2)
    vmem = pl.BlockSpec(memory_space=pltpu.VMEM)
    smem = pl.BlockSpec(memory_space=pltpu.SMEM)
    dma = pltpu.SemaphoreType.DMA((parts,))
    logits, sums = pl.pallas_call(
        functools.partial(main_kernel, parts, count, kr, bs, classes, cp, rp, parts * own),
        out_shape=(
            jax.ShapeDtypeStruct((cp, own), F32),
            jax.ShapeDtypeStruct((used, 128), F32),
        ),
        in_specs=[smem] * 4 + [pl.BlockSpec(memory_space=pl.ANY)] + [vmem] * 4,
        out_specs=(vmem, vmem),
        scratch_shapes=[
            pltpu.VMEM((parts, 8, 128), jnp.int32),
            pltpu.VMEM((parts, 8, 128), jnp.int32),
            pltpu.VMEM((parts, bs, width), BF16),
            pltpu.VMEM((table, bs, width), BF16),
            pltpu.VMEM((table, bs, width), BF16),
            pltpu.VMEM((count, kr, bs, bs), BF16),
            pltpu.VMEM((kr + 1, bs, bs), F32),
            pltpu.VMEM((own, table * bs), BF16),
            pltpu.VMEM((parts * rp, 128), F32),
            pltpu.VMEM((parts, rp, 128), F32),
            pltpu.VMEM((parts * rp, 128), F32),
            pltpu.VMEM((hidden, width), BF16),
            pltpu.VMEM((cw, hidden), F32),
            pltpu.VMEM((cp, hidden), BF16),
            pltpu.VMEM((hidden, cp), BF16),
            pltpu.VMEM((cp, own), F32),
            pltpu.VMEM((2 * cp, own), BF16),
            pltpu.VMEM((cp, hidden), F32),
            pltpu.VMEM((hidden, width), F32),
            pltpu.SemaphoreType.DMA((count,)),
            dma, dma, dma, dma, dma, dma,
        ],
        compiler_params=pltpu.CompilerParams(
            collective_id=0, has_side_effects=True, vmem_limit_bytes=62 * 1024 * 1024),
        name="graph_layers",
    )(halo_request, block_cols, prev, last, tiles, features, labels.reshape(count, bs),
      weight_one, weight_two.T)
    logits, one, two = pl.pallas_call(
        functools.partial(place_kernel, classes, cp, hidden),
        out_shape=(
            jax.ShapeDtypeStruct((classes, own), F32),
            jax.ShapeDtypeStruct((width, hidden), F32),
            jax.ShapeDtypeStruct((classes, hidden), F32),
        ),
        in_specs=[vmem, vmem],
        out_specs=(vmem, vmem, vmem),
        name="place_results",
    )(logits, sums)
    return (logits.T, one, two.T)


def solution(mesh):
    placed = (
        P(("grp", "dom"), None),
        P(("grp", "dom"), None, None, None),
        P(("grp", "dom"), None),
        P(("grp", "dom"), None),
        P(("grp", "dom")),
        P(),
        P(),
    )
    return jax.shard_map(
        local,
        mesh=mesh,
        in_specs=placed,
        out_specs=(P(("grp", "dom"), None), P("grp", None), P("grp", None)),
        check_vma=False,
    )
```

time: 105 us -> 74.5 us (0.71)
  Pallas kernels: 90.4 us -> 70.5 us
  local copies, waits for them, and re-layouts: 13.1 us -> 0 us
  other arithmetic: 0.79 us -> 3.09 us
    pallas_call x2, Pallas kernels: 90.4 us -> 70.5 us  [the longest x1 68.5 us: local(): pl.pallas_call(functools.partial(main_kernel, parts, count, kr, bs, class...]
    unnamed x9 -> x0, local copies, waits for them, and re-layouts: 10.3 us -> none
    reduce_max x0 -> x2, other arithmetic: none -> 3.08 us  [the longest x1 1.62 us: local(): prev = jnp.max(jnp.where(same & before, slot[None, None, :] + 1, 0), axis=2)]
    pad x2 -> x0, local copies, waits for them, and re-layouts: 1.56 us -> none  [the longest x1 1.53 us: local(): w2t = jnp.pad(weight_two.T, ((0, cp - classes), (0, 0)))]
    reshape x1 -> x0, local copies, waits for them, and re-layouts: 1.27 us -> none  [local(): labels.reshape(1, own)]
where the time goes in v2:
time: 74.5 us; the launch traced here: 74.3 us
  Pallas kernels  70.5 us (95%)
  other arithmetic  3.09 us (4%)
    pallas_call x1, Pallas kernels, local(): pl.pallas_call(functools.partial(main_kernel, parts, count, kr, bs, class...  68.5 us
    pallas_call x1, Pallas kernels, local(): pl.pallas_call(functools.partial(place_kernel, classes, cp, hidden), out_...  2.07 us
    reduce_max x1, other arithmetic, local(): prev = jnp.max(jnp.where(same & before, slot[None, None, :] + 1, 0), axis=2)  1.62 us

profile of v2, /device:TPU:0, one launch (start us, length us, event | category | flops | bytes accessed | tf_op | source)
XLA Modules:
  0.0 74.3 jit_solution(13645812143512164293)
XLA Ops:
  0.6 1.5 %select_reduce_fusion.1.last_ref = s32[6,22]{1,0:T(8,128)} fusion(s32[44]{0:T(128)S(1)} %iota_add_fusion, s32[6,44]{1,0:T(8,128)} %cols_ref.1), kind=kLoop, calls=%fused_computation.1 | loop fusion | flops 17292 | bytes 1760 | tf_op jit(solution)/shard_map/reduce_max | solution.py:276
  2.1 1.6 %select_reduce_fusion.prev_ref = s32[6,44]{1,0:T(8,128)} fusion(s32[44]{0:T(128)S(1)} %iota_add_fusion, s32[6,44]{1,0:T(8,128)} %cols_ref.1, pred[44,44]{1,0:T(8,128)(4,1)S(1)} %iota_compare_fusion.1), kind=kLoop, calls=%fused_computation | loop fusion | flops 46200 | bytes 4224 | tf_op jit(solution)/shard_map/reduce_max | solution.py:274
  3.7 68.5 %graph_layers.1 = (f32[176,768]{1,0:T(8,128)}, f32[608,128]{1,0:T(8,128)}) custom-call(s32[1,16]{1,0:T(1,128)} %req_ref.1, s32[6,44]{1,0:T(8,128)} %cols_ref.1, s32[6,44]{1,0:T(8,128)} %select_reduce_fusion.prev_ref, s32[6,22]{1,0:T(8,128)} %select_reduce_fusion.1.last_ref, bf16[6,44,128,128]{3,2,1,0:T(8,128)(2,1)} %bitcast.5, bf16[768,128]{1,0:T(8,128)(2,1)} %feat_ref.1, ...), custom_call_target="tpu_custom_call" | custom-call | tf_op jit(solution)/shard_map/graph_layers/pallas_call | solution.py:280
  72.2 2.1 %place_results.1 = (f32[172,768]{1,0:T(8,128)}, f32[128,256]{1,0:T(8,128)}, f32[172,256]{1,0:T(8,128)}) custom-call(f32[176,768]{1,0:T(8,128)} %get-tuple-element.8.logits_ref, f32[608,128]{1,0:T(8,128)} %get-tuple-element.9.sums_ref), custom_call_target="tpu_custom_call" | custom-call | tf_op jit(solution)/shard_map/place_results/pallas_call | solution.py:316
  (2 shorter events, 0.0 us)

commit v3 on v2

--- a/solution.py
+++ b/solution.py
@@ -33,25 +33,32 @@
 
 def main_kernel(
     parts, count, kr, bs, classes, cp, rp, nodes,
-    req_ref, cols_ref, prev_ref, last_ref, tiles_hbm, feat_ref, lab_ref, w1_ref, w2t_ref,
+    req_ref, cols_ref, colv_ref, tiles_hbm, feat_ref, lab_ref, w1_ref, w2t_ref,
     logits_ref, sums_ref,
     idx_out, idx_in, stage, feat_tab, agg_tab, tiles, chain, adj,
     grads, grads_in, final, w1t, w2pad, w2t, w2, acc, g_hl, two_acc, one_acc,
-    tile_sem, send_sem, idx_sem, feat_sem, agg_sem, rs_sem, ag_sem,
+    plan_v, plan_s, plan_sem, tile_sem, send_sem, idx_sem, feat_sem, agg_sem, rs_sem, ag_sem,
 ):
     grp = lax.axis_index("grp")
     me = lax.axis_index("dom")
     chips = parts // 2
     my_chip = me // 2
     own_pairs = count // 2
+    wide = -(-(count + parts) // 128)
     table = count + parts
     own = count * bs
     hidden = w1_ref.shape[1]
     halves = hidden // 128
     used = halves * cp + hidden
 
-    def peer_at(s):
-        return lax.rem(me + s, parts)
+    def partner(place, t, n):
+        if n & (n - 1):
+            return lax.rem(place + t, n)
+        out, bit = place, 1
+        while bit < n:
+            out += bit * lax.rem(lax.div(t, bit), 2) * (1 - 2 * lax.rem(lax.div(place, bit), 2))
+            bit *= 2
+        return out
 
     def send(src, dst, sem, peer):
         return pltpu.make_async_remote_copy(
@@ -67,7 +74,7 @@
 
     def each_peer(body):
         def step(s, _):
-            body(peer_at(s))
+            body(partner(me, parts - s, parts))
             return 0
 
         lax.fori_loop(1, parts, step, 0)
@@ -81,16 +88,6 @@
     barrier = pltpu.get_barrier_semaphore()
     each_peer(lambda peer: pl.semaphore_signal(
         barrier, inc=1, device_id=(grp, peer), device_id_type=pl.DeviceIdType.MESH))
-    pl.semaphore_wait(barrier, parts - 1)
-
-    def ask(s, _):
-        peer = peer_at(s)
-        idx_out[peer] = jnp.full((8, 128), req_ref[0, peer], jnp.int32)
-        send(idx_out.at[peer], idx_in.at[me], idx_sem, peer).start()
-        return 0
-
-    lax.fori_loop(1, parts, ask, 0)
-    idx_in[me] = jnp.full((8, 128), req_ref[0, me], jnp.int32)
     w1t[...] = w1_ref[...].astype(F32).T.astype(BF16)
     w2pad[...] = jnp.zeros(w2pad.shape, F32)
     w2pad[0:classes, :] = w2t_ref[...].astype(F32)
@@ -98,6 +95,40 @@
     w2[...] = w2pad[...].T[:, 0:cp].astype(BF16)
     for b in range(count):
         feat_tab[b] = feat_ref[b * bs:(b + 1) * bs, :]
+    slot = lax.broadcasted_iota(jnp.int32, (1, kr), 1)
+    lane = lax.broadcasted_iota(jnp.int32, (1, 128), 1)
+    plan_v[...] = jnp.zeros(plan_v.shape, jnp.int32)
+
+    def plan_tile(k, held):
+        out = []
+        for row in range(count):
+            col = cols_ref[row, k]
+            prev, lasts = held[row][0], held[row][1:]
+            same = jnp.logical_and(colv_ref[row:row + 1, :] == col, slot > k)
+            new = [jnp.where(same, k + 1, prev)]
+            for w in range(wide):
+                new.append(jnp.where(lane + 128 * w == col, k + 1, lasts[w]))
+            out.append(tuple(new))
+        return tuple(out)
+
+    none = (jnp.zeros((1, kr), jnp.int32),) + (jnp.zeros((1, 128), jnp.int32),) * wide
+    plans = lax.fori_loop(0, kr, plan_tile, (none,) * count, unroll=4)
+    for row in range(count):
+        plan_v[row:row + 1, 0:kr] = plans[row][0]
+        for w in range(wide):
+            at = 8 * (1 + w) + row
+            plan_v[at:at + 1, :] = plans[row][1 + w]
+    plan_copy = pltpu.make_async_copy(plan_v, plan_s, plan_sem)
+    plan_copy.start()
+    plan_copy.wait()
+    pl.semaphore_wait(barrier, parts - 1)
+
+    def ask(peer):
+        idx_out[peer] = jnp.full((8, 128), req_ref[0, peer], jnp.int32)
+        send(idx_out.at[peer], idx_in.at[me], idx_sem, peer).start()
+
+    each_peer(ask)
+    idx_in[me] = jnp.full((8, 128), req_ref[0, me], jnp.int32)
     each_peer(lambda peer: send(idx_out.at[peer], idx_in.at[me], idx_sem, peer).wait_send())
 
     def pick(peer, tab):
@@ -128,14 +159,15 @@
         tile_copy(row).wait()
 
         def add(k, _):
-            chain[k + 1] = tiles[row, k].astype(F32) + chain[prev_ref[row, k]]
+            chain[k + 1] = tiles[row, k].astype(F32) + chain[plan_s[row, k]]
             return 0
 
         lax.fori_loop(0, kr, add, 0, unroll=4)
         rows = pl.ds(pl.multiple_of(row * bs, bs), bs)
 
         def put(c, _):
-            adj[rows, pl.ds(pl.multiple_of(c * bs, bs), bs)] = chain[last_ref[row, c]].astype(BF16)
+            last = plan_s[8 * (1 + lax.div(c, 128)) + row, lax.rem(c, 128)]
+            adj[rows, pl.ds(pl.multiple_of(c * bs, bs), bs)] = chain[last].astype(BF16)
             return 0
 
         lax.fori_loop(0, table, put, 0, unroll=2)
@@ -175,7 +207,7 @@
         acc[...] += forward(j)
 
     def halo(s, _):
-        chip = lax.rem(my_chip + s, chips)
+        chip = partner(my_chip, s, chips)
         for core in range(2):
             peer = 2 * chip + core
 
@@ -216,13 +248,13 @@
     lax.fori_loop(0, table // 2, backward, 0, unroll=table <= 32)
 
     for h in range(halves):
-        grads[h * cp:(h + 1) * cp, :] = two_acc[:, h * 128:(h + 1) * 128]
-    grads[halves * cp:used, :] = one_acc[...]
+        grads[h * cp:(h + 1) * cp, :] = two_acc[:, h * 128:(h + 1) * 128].astype(BF16)
+    grads[halves * cp:used, :] = one_acc[...].astype(BF16)
     if used < parts * rp:
-        grads[used:, :] = jnp.zeros((parts * rp - used, 128), F32)
+        grads[used:, :] = jnp.zeros((parts * rp - used, 128), BF16)
 
     def share(peer):
-        return pl.ds(pl.multiple_of(peer * rp, 8), rp)
+        return pl.ds(pl.multiple_of(peer * rp, 16), rp)
 
     each_peer(lambda peer: send(
         grads.at[share(peer)], grads_in.at[me], rs_sem, peer).start())
@@ -234,8 +266,8 @@
     each_peer(take)
     each_peer(lambda peer: send(
         grads.at[share(peer)], grads_in.at[me], rs_sem, peer).wait_send())
-    total = lax.fori_loop(0, parts, lambda p, t: t + grads_in[p], jnp.zeros((rp, 128), F32))
-    final[share(me)] = total
+    total = lax.fori_loop(0, parts, lambda p, t: t + grads_in[p].astype(F32), jnp.zeros((rp, 128), F32))
+    final[share(me)] = total.astype(BF16)
     each_peer(lambda peer: send(
         final.at[share(me)], final.at[share(me)], ag_sem, peer).start())
 
@@ -245,7 +277,7 @@
     each_peer(take_total)
     each_peer(lambda peer: send(
         final.at[share(me)], final.at[share(me)], ag_sem, peer).wait_send())
-    sums_ref[...] = final[0:used, :]
+    sums_ref[...] = final[0:used, :].astype(F32)
 
 
 def place_kernel(classes, cp, hidden, logits_ref, sums_ref, out_ref, one_ref, two_ref):
@@ -266,14 +298,9 @@
     own = count * bs
     table = count + parts
     used = (hidden // 128) * cp + hidden
-    rp = -(-used // (8 * parts)) * 8
+    rp = -(-used // (16 * parts)) * 16
     tiles = block_tiles.transpose(0, 2, 1, 3)
-    slot = jnp.arange(kr, dtype=jnp.int32)
-    same = block_cols[:, :, None] == block_cols[:, None, :]
-    before = slot[None, None, :] < slot[None, :, None]
-    prev = jnp.max(jnp.where(same & before, slot[None, None, :] + 1, 0), axis=2)
-    here = block_cols[:, None, :] == jnp.arange(table, dtype=jnp.int32)[None, :, None]
-    last = jnp.max(jnp.where(here, slot[None, None, :] + 1, 0), axis=2)
+    plan = (8 * (1 + -(-table // 128)), 128)
     vmem = pl.BlockSpec(memory_space=pltpu.VMEM)
     smem = pl.BlockSpec(memory_space=pltpu.SMEM)
     dma = pltpu.SemaphoreType.DMA((parts,))
@@ -283,7 +310,7 @@
             jax.ShapeDtypeStruct((cp, own), F32),
             jax.ShapeDtypeStruct((used, 128), F32),
         ),
-        in_specs=[smem] * 4 + [pl.BlockSpec(memory_space=pl.ANY)] + [vmem] * 4,
+        in_specs=[smem, smem, vmem, pl.BlockSpec(memory_space=pl.ANY)] + [vmem] * 4,
         out_specs=(vmem, vmem),
         scratch_shapes=[
             pltpu.VMEM((parts, 8, 128), jnp.int32),
@@ -294,9 +321,9 @@
             pltpu.VMEM((count, kr, bs, bs), BF16),
             pltpu.VMEM((kr + 1, bs, bs), F32),
             pltpu.VMEM((own, table * bs), BF16),
-            pltpu.VMEM((parts * rp, 128), F32),
-            pltpu.VMEM((parts, rp, 128), F32),
-            pltpu.VMEM((parts * rp, 128), F32),
+            pltpu.VMEM((parts * rp, 128), BF16),
+            pltpu.VMEM((parts, rp, 128), BF16),
+            pltpu.VMEM((parts * rp, 128), BF16),
             pltpu.VMEM((hidden, width), BF16),
             pltpu.VMEM((cw, hidden), F32),
             pltpu.VMEM((cp, hidden), BF16),
@@ -305,13 +332,16 @@
             pltpu.VMEM((2 * cp, own), BF16),
             pltpu.VMEM((cp, hidden), F32),
             pltpu.VMEM((hidden, width), F32),
+            pltpu.VMEM(plan, jnp.int32),
+            pltpu.SMEM(plan, jnp.int32),
+            pltpu.SemaphoreType.DMA,
             pltpu.SemaphoreType.DMA((count,)),
             dma, dma, dma, dma, dma, dma,
         ],
         compiler_params=pltpu.CompilerParams(
             collective_id=0, has_side_effects=True, vmem_limit_bytes=62 * 1024 * 1024),
         name="graph_layers",
-    )(halo_request, block_cols, prev, last, tiles, features, labels.reshape(count, bs),
+    )(halo_request, block_cols, block_cols, tiles, features, labels.reshape(count, bs),
       weight_one, weight_two.T)
     logits, one, two = pl.pallas_call(
         functools.partial(place_kernel, classes, cp, hidden),

time: 74.5 us -> 65.3 us (0.88)
  Pallas kernels: 70.5 us -> 64.5 us
  other arithmetic: 3.09 us -> 0 us
    pallas_call x1, Pallas kernels: 68.5 us -> 62.5 us  [local(): pl.pallas_call(functools.partial(main_kernel, parts, count, kr, bs, class...]
    reduce_max x2 -> x0, other arithmetic: 3.08 us -> none  [the longest x1 1.62 us: local(): prev = jnp.max(jnp.where(same & before, slot[None, None, :] + 1, 0), axis=2)]
where the time goes in v3:
time: 65.3 us; the launch traced here: 65.2 us
  Pallas kernels  64.5 us (99%)
    pallas_call x1, Pallas kernels, local(): pl.pallas_call(functools.partial(main_kernel, parts, count, kr, bs, class...  62.5 us
    pallas_call x1, Pallas kernels, local(): pl.pallas_call(functools.partial(place_kernel, classes, cp, hidden), out_...  2.07 us

profile of v3, /device:TPU:0, one launch (start us, length us, event | category | flops | bytes accessed | tf_op | source)
XLA Modules:
  0.0 65.2 jit_solution(1397257107914249599)
XLA Ops:
  0.6 62.5 %graph_layers.1 = (f32[176,768]{1,0:T(8,128)}, f32[608,128]{1,0:T(8,128)}) custom-call(s32[1,16]{1,0:T(1,128)} %req_ref.1, s32[6,44]{1,0:T(8,128)} %colv_ref.1, s32[6,44]{1,0:T(8,128)} %colv_ref.1, bf16[6,44,128,128]{3,2,1,0:T(8,128)(2,1)} %bitcast.5, bf16[768,128]{1,0:T(8,128)(2,1)} %feat_ref.1, s32[6,128]{1,0:T(8,128)} %bitcast.7, ...), custom_call_target="tpu_custom_call" | custom-call | tf_op jit(solution)/shard_map/graph_layers/pallas_call | solution.py:307
  63.1 2.1 %place_results.1 = (f32[172,768]{1,0:T(8,128)}, f32[128,256]{1,0:T(8,128)}, f32[172,256]{1,0:T(8,128)}) custom-call(f32[176,768]{1,0:T(8,128)} %get-tuple-element.8.logits_ref, f32[608,128]{1,0:T(8,128)} %get-tuple-element.9.sums_ref), custom_call_target="tpu_custom_call" | custom-call | tf_op jit(solution)/shard_map/place_results/pallas_call | solution.py:346

commit v4 on v3

--- a/solution.py
+++ b/solution.py
@@ -32,12 +32,13 @@
 
 
 def main_kernel(
-    parts, count, kr, bs, classes, cp, rp, nodes,
+    parts, count, kr, bs, classes, cp, nodes,
     req_ref, cols_ref, colv_ref, tiles_hbm, feat_ref, lab_ref, w1_ref, w2t_ref,
     logits_ref, sums_ref,
     idx_out, idx_in, stage, feat_tab, agg_tab, tiles, chain, adj,
-    grads, grads_in, final, w1t, w2pad, w2t, w2, acc, g_hl, two_acc, one_acc,
-    plan_v, plan_s, plan_sem, tile_sem, send_sem, idx_sem, feat_sem, agg_sem, rs_sem, ag_sem,
+    part_two, in_two, sum_two, part_one, in_one, sum_one, terms, w1t, w2pad, w2t, w2, acc, g_hl, two_acc, one_acc,
+    plan_v, plan_s, plan_sem, tile_sem, send_sem, idx_sem, feat_sem, agg_sem,
+    rs_two, ag_two, rs_one, ag_one, out_rs_two, out_ag_two, out_rs_one, out_ag_one,
 ):
     grp = lax.axis_index("grp")
     me = lax.axis_index("dom")
@@ -60,9 +61,9 @@
             bit *= 2
         return out
 
-    def send(src, dst, sem, peer):
+    def send(src, dst, sem, peer, out_sem=send_sem):
         return pltpu.make_async_remote_copy(
-            src_ref=src, dst_ref=dst, send_sem=send_sem.at[peer], recv_sem=sem.at[me],
+            src_ref=src, dst_ref=dst, send_sem=out_sem.at[peer], recv_sem=sem.at[me],
             device_id=(grp, peer), device_id_type=pl.DeviceIdType.MESH,
         )
 
@@ -235,49 +236,84 @@
     two_acc[...] = jnp.zeros(two_acc.shape, F32)
     one_acc[...] = jnp.zeros(one_acc.shape, F32)
 
-    def backward(j, _):
+    def backward_two(j):
+        pre = dot_nt(w1t[...], pair_agg(j))
+        term = split_rows(fold_rows(dot(g_hl[...], pair_cols(j)), cp))
+        two_acc[...] += fold_rows(dot_nt(term, jnp.maximum(pre, 0.0).astype(BF16)), cp)
+        return term
+
+    def backward_one(j, term):
         agg = pair_agg(j)
         pre = dot_nt(w1t[...], agg)
-        term = split_rows(fold_rows(dot(g_hl[...], pair_cols(j)), cp))
-        two_acc[...] += fold_rows(dot_nt(term, jnp.maximum(pre, 0.0).astype(BF16)), cp)
         grad_hidden = dot(w2[...], term[:cp]) + dot(w2[...], term[cp:])
         grad_pre = jnp.where(pre > 0.0, grad_hidden, 0.0)
         one_acc[...] += fold_rows(dot(split_rows(grad_pre), agg), hidden)
+
+    def share(rows, peer):
+        return pl.ds(pl.multiple_of(peer * rows, 16), rows)
+
+    def scatter(grads, inbox, sem, out_sem):
+        rows = inbox.shape[1]
+        each_peer(lambda peer: send(
+            grads.at[share(rows, peer)], inbox.at[me], sem, peer, out_sem).start())
+        inbox[me] = grads[share(rows, me)]
+
+    def collect(grads, inbox, final, sem, out_sem):
+        rows = inbox.shape[1]
+        each_peer(lambda peer: arrival(inbox.at[peer], sem, peer).wait_recv())
+        total = lax.fori_loop(
+            0, parts, lambda p, t: t + inbox[p].astype(F32), jnp.zeros((rows, 128), F32))
+        final[share(rows, me)] = total.astype(BF16)
+        each_peer(lambda peer: send(
+            grads.at[share(rows, peer)], inbox.at[me], sem, peer, out_sem).wait_send())
+
+    def hand_round(final, rows, sem, out_sem):
+        each_peer(lambda peer: send(
+            final.at[share(rows, me)], final.at[share(rows, me)], sem, peer, out_sem).start())
+
+    def gather(final, rows, sem, out_sem):
+        each_peer(lambda peer: arrival(final.at[share(rows, peer)], sem, peer).wait_recv())
+        each_peer(lambda peer: send(
+            final.at[share(rows, me)], final.at[share(rows, me)], sem, peer, out_sem).wait_send())
+
+    rows_two, rows_one = in_two.shape[1], in_one.shape[1]
+    pairs = table // 2
+    keep = terms.shape[0] == pairs
+
+    def first_pass(j, _):
+        term = backward_two(j)
+        if keep:
+            terms[j] = term
+        else:
+            backward_one(j, term)
         return 0
 
-    lax.fori_loop(0, table // 2, backward, 0, unroll=table <= 32)
-
+    lax.fori_loop(0, pairs, first_pass, 0, unroll=keep)
     for h in range(halves):
-        grads[h * cp:(h + 1) * cp, :] = two_acc[:, h * 128:(h + 1) * 128].astype(BF16)
-    grads[halves * cp:used, :] = one_acc[...].astype(BF16)
-    if used < parts * rp:
-        grads[used:, :] = jnp.zeros((parts * rp - used, 128), BF16)
-
-    def share(peer):
-        return pl.ds(pl.multiple_of(peer * rp, 16), rp)
-
-    each_peer(lambda peer: send(
-        grads.at[share(peer)], grads_in.at[me], rs_sem, peer).start())
-    grads_in[me] = grads[share(me)]
-
-    def take(peer):
-        arrival(grads_in.at[peer], rs_sem, peer).wait_recv()
-
-    each_peer(take)
-    each_peer(lambda peer: send(
-        grads.at[share(peer)], grads_in.at[me], rs_sem, peer).wait_send())
-    total = lax.fori_loop(0, parts, lambda p, t: t + grads_in[p].astype(F32), jnp.zeros((rp, 128), F32))
-    final[share(me)] = total.astype(BF16)
-    each_peer(lambda peer: send(
-        final.at[share(me)], final.at[share(me)], ag_sem, peer).start())
-
-    def take_total(peer):
-        arrival(final.at[share(peer)], ag_sem, peer).wait_recv()
-
-    each_peer(take_total)
-    each_peer(lambda peer: send(
-        final.at[share(me)], final.at[share(me)], ag_sem, peer).wait_send())
-    sums_ref[...] = final[0:used, :].astype(F32)
+        part_two[h * cp:(h + 1) * cp, :] = two_acc[:, h * 128:(h + 1) * 128].astype(BF16)
+    if halves * cp < parts * rows_two:
+        part_two[halves * cp:, :] = jnp.zeros((parts * rows_two - halves * cp, 128), BF16)
+    scatter(part_two, in_two, rs_two, out_rs_two)
+
+    if keep:
+        def second_pass(j, _):
+            backward_one(j, terms[j])
+            return 0
+
+        lax.fori_loop(0, pairs, second_pass, 0, unroll=True)
+    part_one[0:hidden, :] = one_acc[...].astype(BF16)
+    if hidden < parts * rows_one:
+        part_one[hidden:, :] = jnp.zeros((parts * rows_one - hidden, 128), BF16)
+    scatter(part_one, in_one, rs_one, out_rs_one)
+
+    collect(part_two, in_two, sum_two, rs_two, out_rs_two)
+    hand_round(sum_two, rows_two, ag_two, out_ag_two)
+    collect(part_one, in_one, sum_one, rs_one, out_rs_one)
+    hand_round(sum_one, rows_one, ag_one, out_ag_one)
+    gather(sum_two, rows_two, ag_two, out_ag_two)
+    sums_ref[0:halves * cp, :] = sum_two[0:halves * cp, :].astype(F32)
+    gather(sum_one, rows_one, ag_one, out_ag_one)
+    sums_ref[halves * cp:used, :] = sum_one[0:hidden, :].astype(F32)
 
 
 def place_kernel(classes, cp, hidden, logits_ref, sums_ref, out_ref, one_ref, two_ref):
@@ -298,14 +334,15 @@
     own = count * bs
     table = count + parts
     used = (hidden // 128) * cp + hidden
-    rp = -(-used // (16 * parts)) * 16
+    rows_two = -(-((hidden // 128) * cp) // (16 * parts)) * 16
+    rows_one = -(-hidden // (16 * parts)) * 16
     tiles = block_tiles.transpose(0, 2, 1, 3)
     plan = (8 * (1 + -(-table // 128)), 128)
     vmem = pl.BlockSpec(memory_space=pltpu.VMEM)
     smem = pl.BlockSpec(memory_space=pltpu.SMEM)
     dma = pltpu.SemaphoreType.DMA((parts,))
     logits, sums = pl.pallas_call(
-        functools.partial(main_kernel, parts, count, kr, bs, classes, cp, rp, parts * own),
+        functools.partial(main_kernel, parts, count, kr, bs, classes, cp, parts * own),
         out_shape=(
             jax.ShapeDtypeStruct((cp, own), F32),
             jax.ShapeDtypeStruct((used, 128), F32),
@@ -321,9 +358,13 @@
             pltpu.VMEM((count, kr, bs, bs), BF16),
             pltpu.VMEM((kr + 1, bs, bs), F32),
             pltpu.VMEM((own, table * bs), BF16),
-            pltpu.VMEM((parts * rp, 128), BF16),
-            pltpu.VMEM((parts, rp, 128), BF16),
-            pltpu.VMEM((parts * rp, 128), BF16),
+            pltpu.VMEM((parts * rows_two, 128), BF16),
+            pltpu.VMEM((parts, rows_two, 128), BF16),
+            pltpu.VMEM((parts * rows_two, 128), BF16),
+            pltpu.VMEM((parts * rows_one, 128), BF16),
+            pltpu.VMEM((parts, rows_one, 128), BF16),
+            pltpu.VMEM((parts * rows_one, 128), BF16),
+            pltpu.VMEM((table // 2 if table <= 32 else 1, 2 * cp, 2 * bs), BF16),
             pltpu.VMEM((hidden, width), BF16),
             pltpu.VMEM((cw, hidden), F32),
             pltpu.VMEM((cp, hidden), BF16),
@@ -336,7 +377,8 @@
             pltpu.SMEM(plan, jnp.int32),
             pltpu.SemaphoreType.DMA,
             pltpu.SemaphoreType.DMA((count,)),
-            dma, dma, dma, dma, dma, dma,
+            dma, dma, dma, dma,
+            dma, dma, dma, dma, dma, dma, dma, dma,
         ],
         compiler_params=pltpu.CompilerParams(
             collective_id=0, has_side_effects=True, vmem_limit_bytes=62 * 1024 * 1024),

time: 65.3 us -> 62.1 us (0.951)
  Pallas kernels: 64.5 us -> 61.3 us
    pallas_call x1, Pallas kernels: 62.5 us -> 59.2 us  [local(): pl.pallas_call(functools.partial(main_kernel, parts, count, kr, bs, class...]
where the time goes in v4:
time: 62.1 us; the launch traced here: 62 us
  Pallas kernels  61.3 us (99%)
  between operations  0.64 us (1%)
    pallas_call x1, Pallas kernels, local(): pl.pallas_call(functools.partial(main_kernel, parts, count, kr, bs, class...  59.2 us
    pallas_call x1, Pallas kernels, local(): pl.pallas_call(functools.partial(place_kernel, classes, cp, hidden), out_...  2.07 us

profile of v4, /device:TPU:0, one launch (start us, length us, event | category | flops | bytes accessed | tf_op | source)
XLA Modules:
  0.0 62.0 jit_solution(8980703864154296808)
XLA Ops:
  0.6 59.2 %graph_layers.1 = (f32[176,768]{1,0:T(8,128)}, f32[608,128]{1,0:T(8,128)}) custom-call(s32[1,16]{1,0:T(1,128)} %req_ref.1, s32[6,44]{1,0:T(8,128)} %colv_ref.1, s32[6,44]{1,0:T(8,128)} %colv_ref.1, bf16[6,44,128,128]{3,2,1,0:T(8,128)(2,1)} %bitcast.5, bf16[768,128]{1,0:T(8,128)(2,1)} %feat_ref.1, s32[6,128]{1,0:T(8,128)} %bitcast.7, ...), custom_call_target="tpu_custom_call" | custom-call | tf_op jit(solution)/shard_map/graph_layers/pallas_call | solution.py:344
  59.9 2.1 %place_results.1 = (f32[172,768]{1,0:T(8,128)}, f32[128,256]{1,0:T(8,128)}, f32[172,256]{1,0:T(8,128)}) custom-call(f32[176,768]{1,0:T(8,128)} %get-tuple-element.8.logits_ref, f32[608,128]{1,0:T(8,128)} %get-tuple-element.9.sums_ref), custom_call_target="tpu_custom_call" | custom-call | tf_op jit(solution)/shard_map/place_results/pallas_call | solution.py:388

commit v5 on v4

--- a/solution.py
+++ b/solution.py
@@ -52,14 +52,33 @@
     halves = hidden // 128
     used = halves * cp + hidden
 
-    def partner(place, t, n):
+    def flips(place, n):
+        bits = [1 << b for b in range(n.bit_length() - 1)]
+        return [(bit, bit - 2 * bit * lax.rem(lax.div(place, bit), 2)) for bit in bits]
+
+    my_flips, chip_flips = flips(me, parts), flips(my_chip, chips)
+
+    def partner(place, place_flips, t, n):
         if n & (n - 1):
             return lax.rem(place + t, n)
-        out, bit = place, 1
-        while bit < n:
-            out += bit * lax.rem(lax.div(t, bit), 2) * (1 - 2 * lax.rem(lax.div(place, bit), 2))
-            bit *= 2
+        out = place
+        for bit, change in place_flips:
+            if isinstance(t, int):
+                out = out + change if t & bit else out
+            else:
+                out += lax.rem(lax.div(t, bit), 2) * change
         return out
+
+    def each_far(body, unroll=parts <= 16):
+        def step(s, _):
+            body(partner(me, my_flips, parts - s, parts))
+            return 0
+
+        if unroll:
+            for s in range(1, parts):
+                step(s, 0)
+        else:
+            lax.fori_loop(1, parts, step, 0)
 
     def send(src, dst, sem, peer, out_sem=send_sem):
         return pltpu.make_async_remote_copy(
@@ -75,7 +94,7 @@
 
     def each_peer(body):
         def step(s, _):
-            body(partner(me, parts - s, parts))
+            body(lax.rem(me + s, parts))
             return 0
 
         lax.fori_loop(1, parts, step, 0)
@@ -128,7 +147,7 @@
         idx_out[peer] = jnp.full((8, 128), req_ref[0, peer], jnp.int32)
         send(idx_out.at[peer], idx_in.at[me], idx_sem, peer).start()
 
-    each_peer(ask)
+    each_far(ask)
     idx_in[me] = jnp.full((8, 128), req_ref[0, me], jnp.int32)
     each_peer(lambda peer: send(idx_out.at[peer], idx_in.at[me], idx_sem, peer).wait_send())
 
@@ -146,7 +165,7 @@
             stage[peer] = pick(peer, tab)
             send(stage.at[peer], tab.at[count + me], sem, peer).start()
 
-        each_peer(go)
+        each_far(go, False)
         tab[count + me] = pick(me, tab)
 
     def sent(tab, sem):
@@ -208,7 +227,7 @@
         acc[...] += forward(j)
 
     def halo(s, _):
-        chip = partner(my_chip, s, chips)
+        chip = partner(my_chip, chip_flips, s, chips)
         for core in range(2):
             peer = 2 * chip + core
 
@@ -254,7 +273,7 @@
 
     def scatter(grads, inbox, sem, out_sem):
         rows = inbox.shape[1]
-        each_peer(lambda peer: send(
+        each_far(lambda peer: send(
             grads.at[share(rows, peer)], inbox.at[me], sem, peer, out_sem).start())
         inbox[me] = grads[share(rows, me)]
 
@@ -268,7 +287,7 @@
             grads.at[share(rows, peer)], inbox.at[me], sem, peer, out_sem).wait_send())
 
     def hand_round(final, rows, sem, out_sem):
-        each_peer(lambda peer: send(
+        each_far(lambda peer: send(
             final.at[share(rows, me)], final.at[share(rows, me)], sem, peer, out_sem).start())
 
     def gather(final, rows, sem, out_sem):

time: 62.1 us -> 60.2 us (0.969)
  Pallas kernels: 61.3 us -> 59.4 us
    pallas_call x1, Pallas kernels: 59.2 us -> 57.3 us  [local(): pl.pallas_call(functools.partial(main_kernel, parts, count, kr, bs, class...]
where the time goes in v5:
time: 60.2 us; the launch traced here: 60 us
  Pallas kernels  59.4 us (99%)
  between operations  0.64 us (1%)
    pallas_call x1, Pallas kernels, local(): pl.pallas_call(functools.partial(main_kernel, parts, count, kr, bs, class...  57.3 us
    pallas_call x1, Pallas kernels, local(): pl.pallas_call(functools.partial(place_kernel, classes, cp, hidden), out_...  2.07 us

profile of v5, /device:TPU:0, one launch (start us, length us, event | category | flops | bytes accessed | tf_op | source)
XLA Modules:
  0.0 60.0 jit_solution(15507156403735479900)
XLA Ops:
  0.6 57.3 %graph_layers.1 = (f32[176,768]{1,0:T(8,128)}, f32[608,128]{1,0:T(8,128)}) custom-call(s32[1,16]{1,0:T(1,128)} %req_ref.1, s32[6,44]{1,0:T(8,128)} %colv_ref.1, s32[6,44]{1,0:T(8,128)} %colv_ref.1, bf16[6,44,128,128]{3,2,1,0:T(8,128)(2,1)} %bitcast.5, bf16[768,128]{1,0:T(8,128)(2,1)} %feat_ref.1, s32[6,128]{1,0:T(8,128)} %bitcast.7, ...), custom_call_target="tpu_custom_call" | custom-call | tf_op jit(solution)/shard_map/graph_layers/pallas_call | solution.py:363
  58.0 2.1 %place_results.1 = (f32[172,768]{1,0:T(8,128)}, f32[128,256]{1,0:T(8,128)}, f32[172,256]{1,0:T(8,128)}) custom-call(f32[176,768]{1,0:T(8,128)} %get-tuple-element.8.logits_ref, f32[608,128]{1,0:T(8,128)} %get-tuple-element.9.sums_ref), custom_call_target="tpu_custom_call" | custom-call | tf_op jit(solution)/shard_map/place_results/pallas_call | solution.py:407
